TPU v7x, 256 devices: a whole 4x4x8 slice. The times are simulated.
256 devices in a mesh: samp: 8 (over z_hi, core), seq: 32 (over x, y, z_lo).
Axes of the slice: x: 4, y: 4, z: 8 (z_hi: 4, z_lo: 2; z = z_hi * 2 + z_lo), core: 2. Of those that a mesh axis runs over, the one named last changes fastest.
Arguments:
- atom_act: bfloat16 [16, 12288, 128], P('samp', 'seq'), may hold values from -6 to 6
- atom_gain: float32 [128], replicated, may hold values from 0.25 to 1.75
- atom_query: bfloat16 [128, 128], replicated, may hold values from -0.5 to 0.5
- atom_keyval: bfloat16 [128, 256], replicated, may hold values from -0.5 to 0.5
- atom_output: bfloat16 [128, 128], replicated, may hold values from -0.5 to 0.5
- atom_bias: bfloat16 [4, 384, 32, 128], P(None, 'seq'), may hold values from -4 to 298
- key_range: int32 [384, 2], P('seq'), may hold values from 0 to 12288, as said below
- atom_token: int32 [12288], P('seq'), may hold values from 0 to 1535, as said below
- token_counts: int32 [1536], P('seq'), may hold values from 1 to 15, as said below
- gather_weight: bfloat16 [128, 768], replicated, may hold values from -0.5 to 0.5
- token_gain: float32 [768], replicated, may hold values from 0.25 to 1.75
- token_query: bfloat16 [768, 768], replicated, may hold values from -0.21875 to 0.21875
- token_keyval: bfloat16 [768, 1536], replicated, may hold values from -0.21875 to 0.21875
- token_output: bfloat16 [768, 768], replicated, may hold values from -0.21875 to 0.21875
- pair_bias: bfloat16 [16, 1536, 1536], P('samp', 'seq'), may hold values from -4 to 298
- trans_gain: float32 [768], replicated, may hold values from 0.25 to 1.75
- trans_gate_up: bfloat16 [768, 3072], replicated, may hold values from -0.21875 to 0.21875
- trans_down: bfloat16 [1536, 768], replicated, may hold values from -0.15625 to 0.15625
- back_weight: bfloat16 [768, 128], replicated, may hold values from -0.21875 to 0.21875
Outputs:
- atom_out: bfloat16 [16, 12288, 128], P('samp', 'seq')
- token_out: bfloat16 [16, 1536, 768], P('samp', 'seq')
Inputs may be any that keep to these rules, and one draw needn't show every extreme that they name: max(0, 32 * b - 48) <= key_range[b, 0] <= 32 * b and 32 * b + 32 <= key_range[b, 1] <= min(12288, 32 * b + 80). atom_token never falls along the atoms; atom a belongs to token a // 8 or a // 8 - 1. token_counts[t] is the number of atoms a with atom_token[a] = t.
All inputs are finite; a program needn't handle non-finite values.
Results may differ from a plain program's by a relative error of at most 0.025.
Values may be sent and summed in bfloat16 or wider, within the bound.
No kernel may reach another device: no remote copies, remote signals or barrier semaphores. Data moves between devices by JAX's collectives and lax.ppermute only.
A program may use at most 128 MiB of HBM per device.

v0:
```python
import math
import jax
import jax.numpy as jnp
from jax import lax
from jax.sharding import PartitionSpec as P

AH = 4
HEADS = 16
WQ = 32
WK = 128
EDGE = 48
EPSILON = 1e-05
NEGATIVE = -1e30


def extended(cells, sides, width):
    for axis, dim in sides:
        count = lax.axis_size(axis)
        ends = count - 1
        head = lax.slice_in_dim(cells, 0, width, axis=dim)
        tail = lax.slice_in_dim(cells, cells.shape[dim] - width, cells.shape[dim], axis=dim)
        cells = jnp.concatenate(
            [
                lax.ppermute(tail, axis, [(i, (i + 1) % count) for i in range(ends)]),
                cells,
                lax.ppermute(head, axis, [((i + 1) % count, i) for i in range(ends)]),
            ],
            axis=dim,
        )
    return cells


def passed_along(value, axis, by):
    devices = lax.axis_size(axis)
    pairs = [(i, i + by) for i in range(devices) if 0 <= i + by < devices]
    return lax.ppermute(value, axis, pairs)


def layer_norm(values, gain_vector):
    widened = values.astype(jnp.float32)
    centred = widened - jnp.mean(widened, axis=-1, keepdims=True)
    variance = jnp.mean(centred * centred, axis=-1, keepdims=True)
    return (centred * lax.rsqrt(variance + EPSILON) * gain_vector).astype(jnp.bfloat16)


def softmax_rows(scores):
    maxima = jnp.max(scores, axis=-1, keepdims=True)
    exponent = jnp.exp(scores - maxima)
    return exponent / jnp.sum(exponent, axis=-1, keepdims=True)


def project(values, weight):
    return jnp.einsum("sac,cd->sad", values, weight, preferred_element_type=jnp.float32)


def make_attend(query_heads, bias_rows, head_count, head_size, score_scale):

    def attend(running, keyval_piece, first_key):
        best_score, row_total, value_sum = running
        sample_count = keyval_piece.shape[0]
        piece_rows = keyval_piece.shape[1]
        key_heads = keyval_piece[:, :, 0].reshape(sample_count, piece_rows, head_count, head_size)
        value_heads = keyval_piece[:, :, 1].reshape(sample_count, piece_rows, head_count, head_size)
        piece_scores = jnp.einsum(
            "sqhd,skhd->shqk", query_heads, key_heads, preferred_element_type=jnp.float32
        )
        piece_scores = piece_scores * score_scale + bias_rows.astype(jnp.float32)[None]
        new_best = jnp.maximum(best_score, jnp.max(piece_scores, axis=-1))
        exponent = jnp.exp(piece_scores - new_best[..., None])
        row_total = jnp.sum(exponent, axis=-1)
        value_sum = jnp.einsum(
            "shqk,skhd->shqd",
            exponent.astype(jnp.bfloat16),
            value_heads,
            preferred_element_type=jnp.float32,
        )
        return (new_best, row_total, value_sum)

    return attend


def initial_state(sample_count, head_count, token_rows, head_size):
    return (
        jnp.full((sample_count, head_count, token_rows), NEGATIVE, jnp.float32),
        jnp.zeros((sample_count, head_count, token_rows), jnp.float32),
        jnp.zeros((sample_count, head_count, token_rows, head_size), jnp.float32),
    )


def per_device(
    atom_act,
    atom_gain,
    atom_query,
    atom_keyval,
    atom_output,
    atom_bias,
    key_range,
    atom_token,
    token_counts,
    gather_weight,
    token_gain,
    token_query,
    token_keyval,
    token_output,
    pair_bias,
    trans_gain,
    trans_gate_up,
    trans_down,
    back_weight,
):
    samples, atom_rows, channels = atom_act.shape
    windows = atom_rows // WQ
    head_width = channels // AH
    atom_scale = 1.0 / math.sqrt(head_width)
    normed = layer_norm(atom_act, atom_gain)
    queries = project(normed, atom_query).astype(jnp.bfloat16)
    keyvals = project(normed, atom_keyval).astype(jnp.bfloat16)
    padded = extended(keyvals, (("seq", 1),), EDGE)
    blocks = padded.reshape(samples, windows + 2 * EDGE // WQ, WQ, 2 * channels)
    window_keys = jnp.concatenate(
        [blocks[:, shift_at : shift_at + windows] for shift_at in range(WK // WQ)], axis=2
    )
    key_part = window_keys[..., :channels].reshape(samples, windows, WK, AH, head_width)
    value_part = window_keys[..., channels:].reshape(samples, windows, WK, AH, head_width)
    query_part = queries.reshape(samples, windows, WQ, AH, head_width)
    scores = jnp.einsum(
        "swqhd,swkhd->shwqk", query_part, key_part, preferred_element_type=jnp.float32
    )
    scores = scores * atom_scale + atom_bias.astype(jnp.float32)[None]
    window_base = lax.axis_index("seq") * windows + jnp.arange(windows, dtype=jnp.int32)
    position = WQ * window_base[:, None] - EDGE + jnp.arange(WK, dtype=jnp.int32)[None, :]
    key_valid = (position >= key_range[:, 0:1]) & (position < key_range[:, 1:2])
    scores = jnp.where(key_valid[None, None, :, None, :], scores, NEGATIVE)
    weights = softmax_rows(scores).astype(jnp.bfloat16)
    attended = jnp.einsum(
        "shwqk,swkhd->swqhd", weights, value_part, preferred_element_type=jnp.float32
    )
    attended = attended.astype(jnp.bfloat16).reshape(samples, atom_rows, channels)
    atom_mid = (atom_act.astype(jnp.float32) + project(attended, atom_output)).astype(jnp.bfloat16)
    token_rows = token_counts.shape[0]
    first_token = lax.axis_index("seq") * token_rows
    token_slot = atom_token - first_token
    hidden_atoms = jax.nn.relu(project(atom_mid, gather_weight)).astype(jnp.bfloat16)
    own_table = (token_slot[:, None] == jnp.arange(token_rows, dtype=jnp.int32)[None, :]).astype(
        jnp.bfloat16
    )
    own_sums = jnp.einsum(
        "at,sad->std", own_table, hidden_atoms, preferred_element_type=jnp.float32
    )
    before_table = (token_slot == -1).astype(jnp.bfloat16)
    before_sum = jnp.einsum(
        "a,sad->sd", before_table, hidden_atoms, preferred_element_type=jnp.float32
    )
    arrived = passed_along(before_sum, "seq", -1)
    own_sums = own_sums.at[:, token_rows - 1].add(arrived)
    token_act = (own_sums / token_counts.astype(jnp.float32)[None, :, None]).astype(jnp.bfloat16)
    token_norm = layer_norm(token_act, token_gain)
    token_queries = project(token_norm, token_query).astype(jnp.bfloat16)
    model_width = token_norm.shape[-1]
    head_size = model_width // HEADS
    score_scale = 1.0 / math.sqrt(head_size)
    all_bias = lax.all_gather(pair_bias, "samp", axis=0, tiled=True)
    query_heads = token_queries.reshape(samples, token_rows, HEADS, head_size)
    attend = make_attend(query_heads, all_bias, HEADS, head_size, score_scale)
    initial = initial_state(samples, HEADS, token_rows, head_size)
    token_keyvals = (
        project(token_norm, token_keyval)
        .astype(jnp.bfloat16)
        .reshape(samples, token_rows, 2, model_width)
    )
    best_score, row_total, value_sum = attend(
        initial, lax.all_gather(token_keyvals, "seq", axis=1, tiled=True), jnp.int32(0)
    )
    attended_tokens = (value_sum / row_total[..., None]).astype(jnp.bfloat16)
    merged = jnp.einsum(
        "shqd,hde->sqe",
        attended_tokens,
        token_output.reshape(HEADS, head_size, model_width),
        preferred_element_type=jnp.float32,
    )
    token_mid = (token_act.astype(jnp.float32) + merged).astype(jnp.bfloat16)
    trans_norm = layer_norm(token_mid, trans_gain)
    gate_up = project(trans_norm, trans_gate_up)
    hidden_width = trans_down.shape[0]
    hidden = (jax.nn.silu(gate_up[..., :hidden_width]) * gate_up[..., hidden_width:]).astype(
        jnp.bfloat16
    )
    token_out = (token_mid.astype(jnp.float32) + project(hidden, trans_down)).astype(jnp.bfloat16)
    back_rows = project(token_out, back_weight).astype(jnp.bfloat16)
    previous = passed_along(back_rows[:, token_rows - 1], "seq", 1)
    back_table = jnp.concatenate([previous[:, None], back_rows], axis=1)
    lookup = (
        (token_slot + 1)[:, None] == jnp.arange(token_rows + 1, dtype=jnp.int32)[None, :]
    ).astype(jnp.bfloat16)
    gathered_back = jnp.einsum(
        "at,stc->sac", lookup, back_table, preferred_element_type=jnp.float32
    )
    atom_out = (atom_mid.astype(jnp.float32) + gathered_back).astype(jnp.bfloat16)
    return (atom_out, token_out)


def solution(mesh):
    placed = (
        P("samp", "seq", None),
        P(),
        P(),
        P(),
        P(),
        P(None, "seq", None, None),
        P("seq", None),
        P("seq"),
        P("seq"),
        P(),
        P(),
        P(),
        P(),
        P(),
        P("samp", "seq", None),
        P(),
        P(),
        P(),
        P(),
    )
    return jax.shard_map(
        per_device,
        mesh=mesh,
        in_specs=placed,
        out_specs=(P("samp", "seq", None), P("samp", "seq", None)),
        check_vma=False,
    )
```

profile of v0, /device:TPU:6, one launch (start us, length us, event | category | flops | bytes accessed | tf_op | source)
XLA Modules:
  0.0 380.0 jit_solution(8645867233082741902)
XLA Ops:
  11.1 6.5 %collective-permute-start.1 = (bf16[2,48,256]{2,1,0:T(8,128)(2,1)S(1)}, bf16[2,48,256]{2,1,0:T(8,128)(2,1)S(1)}, u32[]{:S(2)}, u32[]{:S(2)}) collective-permute-start(bf16[2,48,256]{2,1,0:T(8,128)(2,1)S(1)} %get-tuple-element.27), channel_id=1, source_target_pairs={{1,0},{2,1},{3,2},{4,3},{5,4},{6,5},{7,6},{8,7},{9,8},{10,9},{11,1... | collective-permute-start | bytes 147464 | tf_op jit(solution)/shard_map/ppermute | solution.py:26
  17.7 1.9 collective-permute-start
  27.7 2.4 copy.78
  30.1 1.5 copy.77
  31.6 1.6 copy.76
  33.1 1.5 copy.75
  34.7 5.0 %pad_maximum_fusion = bf16[2,12,128,256]{2,3,1,0:T(8,128)(2,1)S(1)} fusion(bf16[2,12,32,256]{2,3,1,0:T(8,128)(2,1)} %copy.78, bf16[2,12,32,256]{2,3,1,0:T(8,128)(2,1)} %copy.77, bf16[2,12,32,256]{2,3,1,0:T(8,128)(2,1)} %copy.76, bf16[2,12,32,256]{2,3,1,0:T(8,128)(2,1)} %copy.75), kind=kLoop, calls=%fused_computation.19 | loop fusion | flops 6291456 | bytes 3145728 | tf_op jit(solution)/shard_map/concatenate | solution.py:120
  41.0 3.2 fusion.99
  44.2 3.2 fusion.20
  47.4 1.5 copy.62
  50.4 1.4 maximum_convert_fusion
  52.1 6.6 %collective-permute-start.2 = (f32[2,768]{1,0:T(2,128)S(1)}, f32[2,768]{1,0:T(2,128)S(1)}, u32[]{:S(2)}, u32[]{:S(2)}) collective-permute-start(f32[2,768]{1,0:T(2,128)S(1)} %bitcast.103), channel_id=1, source_target_pairs={{1,0},{2,1},{3,2},{4,3},{5,4},{6,5},{7,6},{8,7},{9,8},{10,9},{11,1... | collective-permute-start | bytes 18440 | tf_op jit(solution)/shard_map/ppermute | solution.py:36
  62.4 1.6 fusion.33
  64.5 4.5 %convert_element_type.104 = f32[16,48,1536]{2,1,0:T(8,128)} convert(bf16[16,48,1536]{2,1,0:T(8,128)(2,1)} %all-gather.5.cloned.1.call-done) | non-fusion elementwise | flops 1179648 | bytes 7077888 | tf_op jit(solution)/shard_map/convert_element_type | solution.py:67
  69.0 208.9 %all-gather.3.cloned.1.call-done = bf16[2,1536,2,768]{3,2,0,1:T(2,128)(2,1)} async-done(((bf16[2,48,2,768]{3,2,0,1:T(2,128)(2,1)}), bf16[2,1536,2,768]{3,2,0,1:T(2,128)(2,1)}) %all-gather.3.cloned.1.call-update) | async-done | bytes 9437200 | tf_op jit(solution)/shard_map/all_gather | solution.py:172
  277.9 19.5 %fusion.95 = (bf16[2,1536,1,768]{3,2,0,1:T(2,128)(2,1)}, bf16[2,1536,1,768]{3,2,0,1:T(2,128)(2,1)}) fusion(bf16[2,1536,2,768]{3,2,0,1:T(2,128)(2,1)} %all-gather.3.cloned.1.call-done), kind=kLoop, calls=%fused_computation.113 | loop fusion | bytes 18874368 | tf_op jit(solution)/shard_map/slice | solution.py:62
  297.5 22.4 %copy.79 = bf16[2,1536,1,768]{1,3,0,2:T(8,128)(2,1)} copy(bf16[2,1536,1,768]{3,2,0,1:T(2,128)(2,1)} %get-tuple-element.19) | data formatting | bytes 9437184
  319.9 22.4 %copy.65 = bf16[2,1536,1,768]{1,3,0,2:T(8,128)(2,1)} copy(bf16[2,1536,1,768]{3,2,0,1:T(2,128)(2,1)} %get-tuple-element.18) | data formatting | bytes 9437184 | tf_op jit(solution)/shard_map/slice | solution.py:62
  342.3 5.1 %fusion.1 = (f32[2,16,48]{2,1,0:T(8,128)S(1)}, f32[2,16,48,1536]{3,2,1,0:T(8,128)S(1)}) fusion(f32[16,48,1536]{2,1,0:T(8,128)} %convert_element_type.104, bf16[2,1536,16,48]{1,3,2,0:T(8,128)(2,1)} %bitcast.96, bf16[2,48,16,48]{3,2,1,0:T(8,128)(2,1)S(1)} %reshape.172), kind=kOutput, calls=%fused_computation.3 | convolution fusion | flops 233568768 | bytes 19027968 | tf_op jit(solution)/shard_map/sqhd,skhd->shqk/dot_general | solution.py:64
  347.5 2.1 fusion.2
  351.0 8.0 %fusion.100 = (f32[2,48]{1,0:T(2,128)S(1)}, f32[2,48,768]{2,1,0:T(8,128)S(1)}) fusion(bf16[16,48,768,1]{2,1,0,3:T(8,128)(2,1)S(1)} %bitcast.100, bf16[2,1536,16,48]{1,3,2,0:T(8,128)(2,1)} %bitcast.97, f32[2,16,48,1536]{3,2,1,0:T(8,128)} %copy-done.2, f32[2,16,48]{2,1,0:T(8,128)S(1)} %broadcast_maximum_fusion, f32[16,48,1536]{2,1,0:T(8,128)} %convert_element_type.104, ...), kind=kOutput, calls=%fused_computation.118 | convolution fusion | flops 349691808 | bytes 20509056 | tf_op jit(solution)/shard_map/shqd,hde->sqe/dot_general | solution.py:175
  359.2 3.4 fusion.6
  363.8 1.9 collective-permute-start.3
  365.7 6.5 %collective-permute-done.3 = bf16[2,128]{1,0:T(2,128)(2,1)S(1)} collective-permute-done((bf16[2,128]{1,0:T(2,128)(2,1)S(1)}, bf16[2,128]{1,0:T(2,128)(2,1)S(1)}, u32[]{:S(2)}, u32[]{:S(2)}) %collective-permute-start.3) | collective-permute-done | bytes 544 | tf_op jit(solution)/shard_map/ppermute | solution.py:36
  (83 shorter events, 22.6 us)
Async XLA Ops:
  7.2 53.6 %copy-start = (bf16[768,1536]{1,0:T(8,128)(2,1)S(1)}, bf16[768,1536]{1,0:T(8,128)(2,1)}, u32[]{:S(2)}) copy-start(bf16[768,1536]{1,0:T(8,128)(2,1)} %param.33) | copy-start | bytes 7077892
  7.2 17.1 %copy-start.6 = (bf16[4,12,32,128]{3,2,1,0:T(8,128)(2,1)S(1)}, bf16[4,12,32,128]{3,2,1,0:T(8,128)(2,1)}, u32[]{:S(2)}) copy-start(bf16[4,12,32,128]{3,2,1,0:T(8,128)(2,1)} %param.26) | copy-start | bytes 1179652
  7.2 57.3 %all-gather.5.cloned.1.call-start = ((), (), s32[]{:S(2)}) async-start(), calls=%async_computation.1 | async-start | bytes 2654208 | tf_op jit(solution)/shard_map/all_gather | solution.py:162
  11.1 15.5 %collective-permute-start.1 = (bf16[2,48,256]{2,1,0:T(8,128)(2,1)S(1)}, bf16[2,48,256]{2,1,0:T(8,128)(2,1)S(1)}, u32[]{:S(2)}, u32[]{:S(2)}) collective-permute-start(bf16[2,48,256]{2,1,0:T(8,128)(2,1)S(1)} %get-tuple-element.27), channel_id=1, source_target_pairs={{1,0},{2,1},{3,2},{4,3},{5,4},{6,5},{7,6},{8,7},{9,8},{10,9},{11,1... | collective-permute-start | bytes 147464 | tf_op jit(solution)/shard_map/ppermute | solution.py:26
  17.7 9.0 %collective-permute-start = (bf16[2,48,256]{2,1,0:T(8,128)(2,1)S(1)}, bf16[2,48,256]{2,1,0:T(8,128)(2,1)S(1)}, u32[]{:S(2)}, u32[]{:S(2)}) collective-permute-start(bf16[2,48,256]{2,1,0:T(8,128)(2,1)S(1)} %get-tuple-element.26), channel_id=1, source_target_pairs={{0,1},{1,2},{2,3},{3,4},{4,5},{5,6},{6,7},{7,8},{8,9},{9,10},{10,1... | collective-permute-start | bytes 147464 | tf_op jit(solution)/shard_map/ppermute | solution.py:24
  19.6 258.3 %all-gather.3.cloned.1.call-start = ((), (), s32[]{:S(2)}) async-start(), calls=%async_computation | async-start | bytes 9732096 | tf_op jit(solution)/shard_map/all_gather | solution.py:172
  39.7 1.3 copy-start.5
  47.4 2.0 copy-start.3
  50.4 10.4 %copy-start.10 = (f32[768]{0:T(1024)S(1)}, f32[768]{0:T(1024)}, u32[]{:S(2)}) copy-start(f32[768]{0:T(1024)} %param.31) | copy-start | bytes 9220
  52.1 8.0 %collective-permute-start.2 = (f32[2,768]{1,0:T(2,128)S(1)}, f32[2,768]{1,0:T(2,128)S(1)}, u32[]{:S(2)}, u32[]{:S(2)}) collective-permute-start(f32[2,768]{1,0:T(2,128)S(1)} %bitcast.103), channel_id=1, source_target_pairs={{1,0},{2,1},{3,2},{4,3},{5,4},{6,5},{7,6},{8,7},{9,8},{10,9},{11,1... | collective-permute-start | bytes 18440 | tf_op jit(solution)/shard_map/ppermute | solution.py:36
  342.3 5.2 %slice-start = ((s8[4718592]{0:T(1024)(128)(4,1)}), s8[4194304]{0:T(1024)(128)(4,1)S(1)}, s32[]{:S(2)}) async-start(s8[4718592]{0:T(1024)(128)(4,1)} %bitcast.94), calls=%async_computation.2 | async-start | bytes 8388608
  342.3 5.2 %slice-start.1 = ((s8[4718592]{0:T(1024)(128)(4,1)}), s8[524288]{0:T(1024)(128)(4,1)S(1)}, s32[]{:S(2)}) async-start(s8[4718592]{0:T(1024)(128)(4,1)} %bitcast.94), calls=%async_computation.3 | async-start | bytes 1048576
  347.4 3.6 copy-start.2
  347.5 3.5 copy-start.4
  351.0 8.2 %copy-start.9 = (f32[768]{0:T(1024)S(1)}, f32[768]{0:T(1024)}, u32[]{:S(2)}) copy-start(f32[768]{0:T(1024)} %param.36) | copy-start | bytes 9220
  359.2 3.5 copy-start.11
  359.2 14.0 %copy-start.1 = (bf16[768,1536]{1,0:T(8,128)(2,1)S(1)}, bf16[768,1536]{1,0:T(8,128)(2,1)}, u32[]{:S(2)}) copy-start(bf16[768,1536]{1,0:T(8,128)(2,1)} %param.33) | copy-start | bytes 7077892
  362.6 0.9 copy-start.7
  363.6 9.6 %copy-start.8 = (bf16[2,48,768]{2,1,0:T(8,128)(2,1)}, bf16[2,48,768]{2,1,0:T(8,128)(2,1)S(1)}, u32[]{:S(2)}) copy-start(bf16[2,48,768]{2,1,0:T(8,128)(2,1)S(1)} %fusion.30) | copy-start | bytes 442372
  363.8 8.4 %collective-permute-start.3 = (bf16[2,128]{1,0:T(2,128)(2,1)S(1)}, bf16[2,128]{1,0:T(2,128)(2,1)S(1)}, u32[]{:S(2)}, u32[]{:S(2)}) collective-permute-start(bf16[2,128]{1,0:T(2,128)(2,1)S(1)} %bitcast.104), channel_id=1, source_target_pairs={{0,1},{1,2},{2,3},{3,4},{4,5},{5,6},{6,7},{7,8},{8,9},{9,10},{10,1... | collective-permute-start | bytes 1544 | tf_op jit(solution)/shard_map/ppermute | solution.py:36
Sparse Core Ops, SparseCore 0:
  19.7 41.0 all-gather.4
  62.6 215.2 all-gather.2
where the time goes:
time: 382 us; the launch traced here: 380 us
  waiting for transfers between devices  217 us (57%)
  local copies, waits for them, and re-layouts  81.8 us (21%)
  matrix products  32.4 us (8%)
  other arithmetic  17.7 us (5%)
  starting transfers between devices  17.1 us (4%)
  between operations  14.4 us (4%)
    all_gather x1, waiting for transfers between devices, per_device(): lax.all_gather(token_keyvals, 'seq', axis=1, tiled=True)  209 us
    slice x2, local copies, waits for them, and re-layouts, attend(): keyval_piece[:, :, 0]  41.9 us
    unnamed x34, local copies, waits for them, and re-layouts  31.2 us
    dot_general x9, matrix products, project(): jnp.einsum('sac,cd->sad', values, weight, preferred_element_type=jnp.floa...  11.4 us
    ppermute x2, starting transfers between devices, passed_along(): return lax.ppermute(value, axis, pairs)  8.56 us
    dot_general x1, matrix products, per_device(): jnp.einsum('shqd,hde->sqe', attended_tokens, token_output.reshape(HEADS,...  7.96 us
  transfers between devices with their start and end apart: 6, of which 4 were waited for; matrix products, arithmetic and copies ran while one was open for 11% of the time, Pallas kernels for 0%

commit v1 on v0

--- a/solution.py
+++ b/solution.py
@@ -11,6 +11,13 @@
 EDGE = 48
 EPSILON = 1e-05
 NEGATIVE = -1e30
+
+
+def all_by_exchange(x, axis, d):
+    peers = lax.axis_size(axis)
+    parts = jnp.stack([x for _ in range(peers)])
+    parts = lax.all_to_all(parts, axis, split_axis=0, concat_axis=0)
+    return jnp.concatenate(parts, axis=d)
 
 
 def extended(cells, sides, width):
@@ -169,7 +176,7 @@
         .reshape(samples, token_rows, 2, model_width)
     )
     best_score, row_total, value_sum = attend(
-        initial, lax.all_gather(token_keyvals, "seq", axis=1, tiled=True), jnp.int32(0)
+        initial, all_by_exchange(token_keyvals, "seq", 1), jnp.int32(0)
     )
     attended_tokens = (value_sum / row_total[..., None]).astype(jnp.bfloat16)
     merged = jnp.einsum(

time: 382 us -> 309 us (0.81)
  waiting for transfers between devices: 217 us -> 162 us
  local copies, waits for them, and re-layouts: 81.8 us -> 48.3 us
  starting transfers between devices: 17.1 us -> 23.5 us
    all_gather x1 -> x0, waiting for transfers between devices: 209 us -> none  [per_device(): lax.all_gather(token_keyvals, 'seq', axis=1, tiled=True)]
    all_to_all x0 -> x1, waiting for transfers between devices: none -> 102 us  [all_by_exchange(): parts = lax.all_to_all(parts, axis, split_axis=0, concat_axis=0)]
    all_gather x1, waiting for transfers between devices: 0.02 us -> 51 us  [per_device(): all_bias = lax.all_gather(pair_bias, 'samp', axis=0, tiled=True)]
    slice x2, local copies, waits for them, and re-layouts: 41.9 us -> 14.6 us  [attend(): keyval_piece[:, :, 0]]
    unnamed x34 -> x29, local copies, waits for them, and re-layouts: 31.2 us -> 7.33 us
    all_to_all x0 -> x1, starting transfers between devices: none -> 8.97 us  [all_by_exchange(): parts = lax.all_to_all(parts, axis, split_axis=0, concat_axis=0)]
    all_to_all x0 -> x1, local copies, waits for them, and re-layouts: none -> 8.12 us  [all_by_exchange(): parts = lax.all_to_all(parts, axis, split_axis=0, concat_axis=0)]
    slice x0 -> x1, local copies, waits for them, and re-layouts: none -> 6.65 us  [attend(): keyval_piece[:, :, 1]]
  transfers between devices with their start and end apart: 6 -> 6, of which waited for: 4 -> 4; matrix products, arithmetic and copies ran while one was open for 11% -> 4% of each run, Pallas kernels for 0% -> 0%
where the time goes in v1:
time: 309 us; the launch traced here: 304 us
  waiting for transfers between devices  162 us (52%)
  local copies, waits for them, and re-layouts  48.3 us (16%)
  matrix products  34.8 us (11%)
  starting transfers between devices  23.5 us (8%)
  other arithmetic  21 us (7%)
  between operations  14.4 us (5%)
    all_to_all x1, waiting for transfers between devices, all_by_exchange(): parts = lax.all_to_all(parts, axis, split_axis=0, concat_axis=0)  102 us
    all_gather x1, waiting for transfers between devices, per_device(): all_bias = lax.all_gather(pair_bias, 'samp', axis=0, tiled=True)  51 us
    slice x2, local copies, waits for them, and re-layouts, attend(): keyval_piece[:, :, 0]  14.6 us
    dot_general x9, matrix products, project(): jnp.einsum('sac,cd->sad', values, weight, preferred_element_type=jnp.floa...  10.1 us
    all_to_all x1, starting transfers between devices, all_by_exchange(): parts = lax.all_to_all(parts, axis, split_axis=0, concat_axis=0)  8.97 us
    dot_general x1, matrix products, attend(): jnp.einsum('sqhd,skhd->shqk', query_heads, key_heads, preferred_element_t...  8.86 us
    ppermute x2, waiting for transfers between devices, passed_along(): return lax.ppermute(value, axis, pairs)  8.16 us
    all_to_all x1, local copies, waits for them, and re-layouts, all_by_exchange(): parts = lax.all_to_all(parts, axis, split_axis=0, concat_axis=0)  8.12 us
  transfers between devices with their start and end apart: 6, of which 4 were waited for; matrix products, arithmetic and copies ran while one was open for 4% of the time, Pallas kernels for 0%

profile of v1, /device:TPU:6, one launch (start us, length us, event | category | flops | bytes accessed | tf_op | source)
XLA Modules:
  0.0 303.9 jit_solution(11870319395494021159)
XLA Ops:
  11.0 3.8 %collective-permute-start = (bf16[2,48,256]{2,1,0:T(8,128)(2,1)S(1)}, bf16[2,48,256]{2,1,0:T(8,128)(2,1)S(1)}, u32[]{:S(2)}, u32[]{:S(2)}) collective-permute-start(bf16[2,48,256]{2,1,0:T(8,128)(2,1)S(1)} %get-tuple-element.26), channel_id=1, source_target_pairs={{0,1},{1,2},{2,3},{3,4},{4,5},{5,6},{6,7},{7,8},{8,9},{9,10},{10,1... | collective-permute-start | bytes 147464 | tf_op jit(solution)/shard_map/ppermute | solution.py:31
  14.9 5.0 %collective-permute-start.1 = (bf16[2,48,256]{2,1,0:T(8,128)(2,1)S(1)}, bf16[2,48,256]{2,1,0:T(8,128)(2,1)S(1)}, u32[]{:S(2)}, u32[]{:S(2)}) collective-permute-start(bf16[2,48,256]{2,1,0:T(8,128)(2,1)S(1)} %get-tuple-element.27), channel_id=1, source_target_pairs={{1,0},{2,1},{3,2},{4,3},{5,4},{6,5},{7,6},{8,7},{9,8},{10,9},{11,1... | collective-permute-start | bytes 147464 | tf_op jit(solution)/shard_map/ppermute | solution.py:33
  26.7 2.4 copy.79
  33.5 4.8 %pad_maximum_fusion = bf16[2,12,128,256]{2,3,1,0:T(8,128)(2,1)S(1)} fusion(bf16[2,12,32,256]{2,3,1,0:T(8,128)(2,1)} %copy.82, bf16[2,12,32,256]{2,3,1,0:T(8,128)(2,1)} %copy.81, bf16[2,12,32,256]{2,3,1,0:T(8,128)(2,1)} %copy.80, bf16[2,12,32,256]{2,3,1,0:T(8,128)(2,1)} %copy.79), kind=kLoop, calls=%fused_computation.19 | loop fusion | flops 6291456 | bytes 3145728 | tf_op jit(solution)/shard_map/concatenate | solution.py:127
  39.7 3.2 %fusion.99 = (f32[2,4,12,32]{3,2,1,0:T(8,128)S(1)}, f32[2,4,12,32,128]{4,3,2,1,0:T(8,128)}) fusion(bf16[2,12,128,4,32]{2,4,3,1,0:T(8,128)(2,1)} %bitcast.110, bf16[2,12,32,4,32]{4,3,2,1,0:T(4,128)(2,1)} %reshape.173, f32[4,12,32,128]{3,2,1,0:T(8,128)S(1)} %copy-done.5, pred[12,128]{1,0:T(8,128)(4,1)S(1)} %fusion.89), kind=kOutput, calls=%fused_computation.118 | convolution fusion | flops 27132032 | bytes 3356160 | tf_op jit(solution)/shard_map/sub | solution.py:55
  42.9 3.2 %fusion.20 = bf16[2,12,32,4,32]{2,4,3,1,0:T(8,128)(2,1)} fusion(bf16[2,12,128,4,32]{2,4,3,1,0:T(8,128)(2,1)} %bitcast.109, f32[2,4,12,32,128]{4,3,2,1,0:T(8,128)} %get-tuple-element.31, f32[2,4,12,32]{3,2,1,0:T(8,128)S(1)} %get-tuple-element.30), kind=kOutput, calls=%fused_computation.24 | convolution fusion | flops 26050560 | bytes 2568192 | tf_op jit(solution)/shard_map/shwqk,swkhd->swqhd/dot_general | solution.py:142
  46.1 1.5 copy.65
  50.7 3.5 %collective-permute-start.2 = (f32[2,768]{1,0:T(2,128)S(1)}, f32[2,768]{1,0:T(2,128)S(1)}, u32[]{:S(2)}, u32[]{:S(2)}) collective-permute-start(f32[2,768]{1,0:T(2,128)S(1)} %bitcast.111), channel_id=1, source_target_pairs={{1,0},{2,1},{3,2},{4,3},{5,4},{6,5},{7,6},{8,7},{9,8},{10,9},{11,1... | collective-permute-start | bytes 18440 | tf_op jit(solution)/shard_map/ppermute | solution.py:43
  54.6 1.7 collective-permute-done.2
  57.3 4.7 %stack.3 = bf16[32,2,48,2,768]{4,2,3,1,0:T(8,128)(2,1)} broadcast(bf16[2,48,2,768]{3,1,2,0:T(8,128)(2,1)S(1)} %bitcast.107), dimensions={1,2,3,4} | broadcast | bytes 9732096 | tf_op jit(solution)/shard_map/stack | solution.py:18
  62.1 9.0 %all-to-all-start = ((bf16[32,2,48,2,768]{4,2,3,1,0:T(8,128)(2,1)}), bf16[32,2,48,2,768]{4,2,3,1,0:T(8,128)(2,1)}, u32[]{:S(2)}, u32[]{:S(2)}) async-start(bf16[32,2,48,2,768]{4,2,3,1,0:T(8,128)(2,1)} %stack.3), calls=%async_computation | async-start | bytes 18874368 | tf_op jit(solution)/shard_map/all_to_all | solution.py:19
  72.6 51.0 %all-gather.2.cloned.1.call-done = bf16[16,48,1536]{2,1,0:T(8,128)(2,1)} async-done(((bf16[2,48,1536]{2,1,0:T(8,128)(2,1)}), bf16[16,48,1536]{2,1,0:T(8,128)(2,1)}) %all-gather.2.cloned.1.call-update) | async-done | bytes 2359312 | tf_op jit(solution)/shard_map/all_gather | solution.py:169
  123.7 4.4 %convert_element_type.104 = f32[16,48,1536]{2,1,0:T(8,128)} convert(bf16[16,48,1536]{2,1,0:T(8,128)(2,1)} %all-gather.2.cloned.1.call-done) | non-fusion elementwise | flops 1179648 | bytes 7077888 | tf_op jit(solution)/shard_map/convert_element_type | solution.py:74
  128.1 102.2 %all-to-all-done = bf16[32,2,48,2,768]{4,2,3,1,0:T(8,128)(2,1)} async-done(((bf16[32,2,48,2,768]{4,2,3,1,0:T(8,128)(2,1)}), bf16[32,2,48,2,768]{4,2,3,1,0:T(8,128)(2,1)}, u32[]{:S(2)}, u32[]{:S(2)}) %all-to-all-start) | async-done | bytes 9437216 | tf_op jit(solution)/shard_map/all_to_all | solution.py:19
  230.3 8.1 %copy.68 = bf16[32,2,48,2,768]{4,2,0,3,1:T(8,128)(2,1)} copy(bf16[32,2,48,2,768]{4,2,3,1,0:T(8,128)(2,1)} %all-to-all-done) | data formatting | bytes 18874368 | tf_op jit(solution)/shard_map/all_to_all | solution.py:19
  238.4 7.9 %fusion.95 = (bf16[2,1536,1,768]{3,1,2,0:T(8,128)(2,1)}, bf16[2,1536,1,768]{3,1,2,0:T(8,128)(2,1)}) fusion(bf16[2,1536,2,768]{3,1,2,0:T(8,128)(2,1)} %bitcast.101), kind=kLoop, calls=%fused_computation.114 | loop fusion | bytes 18874368 | tf_op jit(solution)/shard_map/slice | solution.py:69
  246.4 6.7 %copy.69 = bf16[2,1536,1,768]{1,3,0,2:T(8,128)(2,1)} copy(bf16[2,1536,1,768]{3,1,2,0:T(8,128)(2,1)} %get-tuple-element.18) | data formatting | bytes 9437184 | tf_op jit(solution)/shard_map/slice | solution.py:69
  253.0 8.9 %fusion.1 = (f32[2,16,48]{2,1,0:T(8,128)S(1)}, f32[2,16,48,1536]{3,2,1,0:T(8,128)}) fusion(f32[16,48,1536]{2,1,0:T(8,128)} %convert_element_type.104, bf16[2,1536,16,48]{1,3,2,0:T(8,128)(2,1)} %bitcast.102, bf16[2,48,16,48]{3,2,1,0:T(8,128)(2,1)S(1)} %reshape.177), kind=kOutput, calls=%fused_computation.3 | convolution fusion | flops 233568768 | bytes 19027968 | tf_op jit(solution)/shard_map/sqhd,skhd->shqk/dot_general | solution.py:71
  261.9 6.7 %copy.71 = bf16[2,1536,1,768]{1,3,0,2:T(8,128)(2,1)} copy(bf16[2,1536,1,768]{3,1,2,0:T(8,128)(2,1)} %get-tuple-element.19) | data formatting | bytes 9437184 | tf_op jit(solution)/shard_map/slice | solution.py:70
  268.5 6.2 %fusion.2 = f32[2,16,48]{2,1,0:T(8,128)S(1)} fusion(f32[2,16,48,1536]{3,2,1,0:T(8,128)} %get-tuple-element.33, f32[2,16,48]{2,1,0:T(8,128)S(1)} %broadcast_maximum_fusion, f32[16,48,1536]{2,1,0:T(8,128)} %convert_element_type.104), kind=kLoop, calls=%fused_computation.4 | loop fusion | flops 9435648 | bytes 14168064 | tf_op jit(solution)/shard_map/reduce_sum | solution.py:77
  274.8 8.0 %fusion.100 = (f32[2,48]{1,0:T(2,128)S(1)}, f32[2,48,768]{2,1,0:T(8,128)S(1)}) fusion(bf16[16,48,768,1]{2,1,0,3:T(8,128)(2,1)S(1)} %bitcast.106, bf16[2,1536,16,48]{1,3,2,0:T(8,128)(2,1)} %bitcast.103, f32[2,16,48,1536]{3,2,1,0:T(8,128)} %get-tuple-element.33, f32[2,16,48]{2,1,0:T(8,128)S(1)} %broadcast_maximum_fusion, ...), kind=kOutput, calls=%fused_computation.119 | convolution fusion | flops 349691808 | bytes 20509056 | tf_op jit(solution)/shard_map/shqd,hde->sqe/dot_general | solution.py:182
  283.0 3.4 %fusion.6 = f32[2,48,3072]{2,1,0:T(8,128)S(1)} fusion(bf16[768,3072]{1,0:T(8,128)(2,1)} %param.37, f32[2,48,768]{2,1,0:T(8,128)S(1)} %get-tuple-element.35, f32[768]{0:T(1024)S(1)} %copy-done.9, f32[2,48]{1,0:T(2,128)S(1)} %add_rsqrt_fusion.1, f32[2,48]{1,0:T(2,128)S(1)} %broadcast_multiply_fusion.1), kind=kOutput, calls=%fused_computation.7 | convolution fusion | flops 453279744 | bytes 6196992 | tf_op jit(solution)/shard_map/sac,cd->sad/dot_general | solution.py:60
  287.6 1.9 collective-permute-start.3
  289.5 6.5 %collective-permute-done.3 = bf16[2,128]{1,0:T(2,128)(2,1)S(1)} collective-permute-done((bf16[2,128]{1,0:T(2,128)(2,1)S(1)}, bf16[2,128]{1,0:T(2,128)(2,1)S(1)}, u32[]{:S(2)}, u32[]{:S(2)}) %collective-permute-start.3) | collective-permute-done | bytes 544 | tf_op jit(solution)/shard_map/ppermute | solution.py:43
  (78 shorter events, 24.6 us)
Async XLA Ops:
  7.2 49.6 %copy-start = (bf16[768,1536]{1,0:T(8,128)(2,1)S(1)}, bf16[768,1536]{1,0:T(8,128)(2,1)}, u32[]{:S(2)}) copy-start(bf16[768,1536]{1,0:T(8,128)(2,1)} %param.33) | copy-start | bytes 7077892
  7.2 17.5 %copy-start.6 = (bf16[4,12,32,128]{3,2,1,0:T(8,128)(2,1)S(1)}, bf16[4,12,32,128]{3,2,1,0:T(8,128)(2,1)}, u32[]{:S(2)}) copy-start(bf16[4,12,32,128]{3,2,1,0:T(8,128)(2,1)} %param.26) | copy-start | bytes 1179652
  11.0 14.6 %collective-permute-start = (bf16[2,48,256]{2,1,0:T(8,128)(2,1)S(1)}, bf16[2,48,256]{2,1,0:T(8,128)(2,1)S(1)}, u32[]{:S(2)}, u32[]{:S(2)}) collective-permute-start(bf16[2,48,256]{2,1,0:T(8,128)(2,1)S(1)} %get-tuple-element.26), channel_id=1, source_target_pairs={{0,1},{1,2},{2,3},{3,4},{4,5},{5,6},{6,7},{7,8},{8,9},{9,10},{10,1... | collective-permute-start | bytes 147464 | tf_op jit(solution)/shard_map/ppermute | solution.py:31
  14.9 10.8 %collective-permute-start.1 = (bf16[2,48,256]{2,1,0:T(8,128)(2,1)S(1)}, bf16[2,48,256]{2,1,0:T(8,128)(2,1)S(1)}, u32[]{:S(2)}, u32[]{:S(2)}) collective-permute-start(bf16[2,48,256]{2,1,0:T(8,128)(2,1)S(1)} %get-tuple-element.27), channel_id=1, source_target_pairs={{1,0},{2,1},{3,2},{4,3},{5,4},{6,5},{7,6},{8,7},{9,8},{10,9},{11,1... | collective-permute-start | bytes 147464 | tf_op jit(solution)/shard_map/ppermute | solution.py:33
  38.4 1.4 copy-start.5
  46.1 2.0 copy-start.2
  49.0 7.7 %copy-start.10 = (f32[768]{0:T(1024)S(1)}, f32[768]{0:T(1024)}, u32[]{:S(2)}) copy-start(f32[768]{0:T(1024)} %param.31) | copy-start | bytes 9220
  50.7 5.5 %collective-permute-start.2 = (f32[2,768]{1,0:T(2,128)S(1)}, f32[2,768]{1,0:T(2,128)S(1)}, u32[]{:S(2)}, u32[]{:S(2)}) collective-permute-start(f32[2,768]{1,0:T(2,128)S(1)} %bitcast.111), channel_id=1, source_target_pairs={{1,0},{2,1},{3,2},{4,3},{5,4},{6,5},{7,6},{8,7},{9,8},{10,9},{11,1... | collective-permute-start | bytes 18440 | tf_op jit(solution)/shard_map/ppermute | solution.py:43
  62.1 9.7 %copy-start.4 = (bf16[768,768]{1,0:T(8,128)(2,1)S(1)}, bf16[768,768]{1,0:T(8,128)(2,1)}, u32[]{:S(2)}) copy-start(bf16[768,768]{1,0:T(8,128)(2,1)} %param.32) | copy-start | bytes 3538948
  62.1 168.2 %all-to-all-start = ((bf16[32,2,48,2,768]{4,2,3,1,0:T(8,128)(2,1)}), bf16[32,2,48,2,768]{4,2,3,1,0:T(8,128)(2,1)}, u32[]{:S(2)}, u32[]{:S(2)}) async-start(bf16[32,2,48,2,768]{4,2,3,1,0:T(8,128)(2,1)} %stack.3), calls=%async_computation | async-start | bytes 18874368 | tf_op jit(solution)/shard_map/all_to_all | solution.py:19
  71.0 52.6 %all-gather.2.cloned.1.call-start = ((), (), s32[]{:S(2)}) async-start(), calls=%async_computation.1 | async-start | bytes 2654208 | tf_op jit(solution)/shard_map/all_gather | solution.py:169
  268.5 6.2 %copy-start.3 = (bf16[768,768]{1,0:T(8,128)(2,1)S(1)}, bf16[768,768]{1,0:T(8,128)(2,1)}, u32[]{:S(2)}) copy-start(bf16[768,768]{1,0:T(8,128)(2,1)} %param.34) | copy-start | bytes 3538948
  274.8 8.2 %copy-start.9 = (f32[768]{0:T(1024)S(1)}, f32[768]{0:T(1024)}, u32[]{:S(2)}) copy-start(f32[768]{0:T(1024)} %param.36) | copy-start | bytes 9220
  283.0 3.5 %copy-start.11 = (bf16[1536,768]{1,0:T(8,128)(2,1)S(1)}, bf16[1536,768]{1,0:T(8,128)(2,1)}, u32[]{:S(2)}) copy-start(bf16[1536,768]{1,0:T(8,128)(2,1)} %param.38) | copy-start | bytes 7077892
  283.0 14.0 %copy-start.1 = (bf16[768,1536]{1,0:T(8,128)(2,1)S(1)}, bf16[768,1536]{1,0:T(8,128)(2,1)}, u32[]{:S(2)}) copy-start(bf16[768,1536]{1,0:T(8,128)(2,1)} %param.33) | copy-start | bytes 7077892
  286.5 0.9 copy-start.7
  287.4 9.6 %copy-start.8 = (bf16[2,48,768]{2,1,0:T(8,128)(2,1)}, bf16[2,48,768]{2,1,0:T(8,128)(2,1)S(1)}, u32[]{:S(2)}) copy-start(bf16[2,48,768]{2,1,0:T(8,128)(2,1)S(1)} %fusion.30) | copy-start | bytes 442372
  287.6 8.4 %collective-permute-start.3 = (bf16[2,128]{1,0:T(2,128)(2,1)S(1)}, bf16[2,128]{1,0:T(2,128)(2,1)S(1)}, u32[]{:S(2)}, u32[]{:S(2)}) collective-permute-start(bf16[2,128]{1,0:T(2,128)(2,1)S(1)} %bitcast.112), channel_id=1, source_target_pairs={{0,1},{1,2},{2,3},{3,4},{4,5},{5,6},{6,7},{7,8},{8,9},{9,10},{10,1... | collective-permute-start | bytes 1544 | tf_op jit(solution)/shard_map/ppermute | solution.py:43
Sparse Core Ops, SparseCore 0:
  73.7 49.9 all-gather.1
